TPU v7x, 512 devices: a whole 4x4x16 slice. The times are simulated.
512 devices in a mesh: bin: 2 (over core), row: 16 (over y, x), col: 16 (over z).
Axes of the slice: x: 4, y: 4, z: 16, core: 2. Of those that a mesh axis runs over, the one named last changes fastest.
Arguments:
- gamma: bfloat16 [4, 2, 2048, 2048], P('bin', None, 'row', 'col'), parts along dimension 0, may hold values from -200 to 200, as said below
- right_side: float32 [4, 2, 2048, 2048], P('bin', None, 'row', 'col'), parts along dimension 0, may hold values from -26 to 26
Outputs:
- solution: float32 [4, 2, 2048, 2048], P('bin', None, 'row', 'col'), parts along dimension 0
- residual: float32 [4, 2, 2048, 2048], P('bin', None, 'row', 'col'), parts along dimension 0
There are 2 independent parts, one for each index of `bin`. A program takes and returns all parts, laid end to end along the dimension named above; each array names one. Nothing has to cross between parts.
Inputs may be any that keep to these rules, and one draw needn't show every extreme that they name: Each bin's gamma is Hermitian (gamma[0] symmetric, gamma[1] antisymmetric) and positive definite.
All inputs are finite; a program needn't handle non-finite values.
Results may differ from a plain program's by a relative error of at most 0.011.
Values may be sent and summed in bfloat16 or wider, within the bound.
A program may use at most 64 MiB of HBM per device.

v0:
```python
import jax
import jax.numpy as jnp
from jax import lax
from jax.sharding import PartitionSpec as P

N = 2048
ITERS = 3


EPS_REL = 0.1


def column_sum(first, second):
    return jnp.sum(first[:, 0] * second[:, 0] + first[:, 1] * second[:, 1], axis=1)


def bin_product(left, right):
    return jnp.einsum("bij,bjk->bik", left, right, preferred_element_type=jnp.float32)


def complex_terms(left, right):
    real_part = bin_product(left[:, 0], right[:, 0]) - bin_product(left[:, 1], right[:, 1])
    imag_part = bin_product(left[:, 0], right[:, 1]) + bin_product(left[:, 1], right[:, 0])
    return (real_part, imag_part)


def curvature_sum(direction, image):
    return lax.psum(column_sum(direction, image), "row")


def spread_cols(values):
    return values[:, None, None, :]


def local(gamma, right_side):
    diagonal_tile = lax.axis_index("row") == lax.axis_index("col")
    diag_sums = jnp.sum(jnp.diagonal(gamma[:, 0], axis1=1, axis2=2).astype(jnp.float32), axis=1)
    local_trace = jnp.where(diagonal_tile, diag_sums, jnp.zeros_like(diag_sums))
    trace_total = lax.psum(local_trace, ("row", "col"))
    damping = (EPS_REL * trace_total / N)[:, None, None]
    bin_count = gamma.shape[0]
    tile_rows = gamma.shape[2]
    tile_cols = right_side.shape[3]
    empty = (
        jnp.zeros((bin_count, tile_rows, tile_cols), jnp.float32),
        jnp.zeros((bin_count, tile_rows, tile_cols), jnp.float32),
    )
    panel = lax.all_gather(gamma, "col", axis=3, tiled=True)
    solution = jnp.zeros_like(right_side)
    residual = right_side
    direction = right_side
    norm_now = lax.psum(column_sum(residual, residual), "row")
    norm_next = norm_now
    for step in range(ITERS):
        lowered = direction.astype(jnp.bfloat16)
        piece = lax.all_gather(lowered, "row", axis=2, tiled=True)
        columns = lax.slice_in_dim(panel, 0, piece.shape[2], axis=3)
        real_part, imag_part = complex_terms(columns, piece)
        real_sum = empty[0] + real_part
        imag_sum = empty[1] + imag_part
        image = jnp.stack(
            [real_sum + damping * direction[:, 0], imag_sum + damping * direction[:, 1]], axis=1
        )
        alpha = norm_now / curvature_sum(direction, image)
        solution = solution + spread_cols(alpha) * direction
        residual = residual - spread_cols(alpha) * image
        if step + 1 < ITERS:
            norm_next = lax.psum(column_sum(residual, residual), "row")
        if step + 1 < ITERS:
            direction = residual + spread_cols(norm_next / norm_now) * direction
            norm_now = norm_next
    return (solution, residual)


def solution(mesh):
    in_specs = (P("bin", None, "row", "col"), P("bin", None, "row", "col"))
    out_specs = (P("bin", None, "row", "col"), P("bin", None, "row", "col"))
    return jax.shard_map(local, mesh=mesh, in_specs=in_specs, out_specs=out_specs, check_vma=False)
```

profile of v0, /device:TPU:33, one launch (start us, length us, event | category | flops | bytes accessed | tf_op | source)
XLA Modules:
  0.0 1017.4 jit_solution(10129960084263872970)
XLA Ops:
  7.2 1.6 copy.19
  8.9 1.6 copy.6
  10.6 0.8 slice.44
  11.4 3.3 copy.14
  14.7 1.9 gather_fusion
  16.7 580.1 %psum.50 = f32[2]{0:T(128)S(1)} all-reduce(f32[2]{0:T(128)S(1)} %broadcast_select_fusion), channel_id=1, replica_groups=mesh['bin'=2,'row'=16,'col'=16] {'row','col'}, use_global_device_ids=true, to_apply=%region_3.4 | all-reduce | flops 2 | bytes 16 | tf_op jit(solution)/shard_map/psum | solution.py:39
  596.9 2.1 fusion.10
  599.1 1.8 fusion.11
  601.6 0.5 add_reduce_fusion.2
  602.0 28.5 %all-reduce = (f32[2,128]{1,0:T(2,128)S(1)}, f32[2,128]{1,0:T(2,128)S(1)}) all-reduce(f32[2,128]{1,0:T(2,128)S(1)} %get-tuple-element.5, f32[2,128]{1,0:T(2,128)S(1)} %get-tuple-element.4), channel_id=1, replica_groups=mesh['bin'=2,'row'=16,'col'=16] {'row'}, use_global_device_ids=true, to_apply=%region_1.2 | all-reduce | flops 512 | bytes 4096 | tf_op jit(solution)/shard_map/psum | solution.py:52
  630.6 29.9 %psum.52 = f32[2,128]{1,0:T(2,128)S(1)} all-reduce(f32[2,128]{1,0:T(2,128)S(1)} %fusion.22), channel_id=1, replica_groups=mesh['bin'=2,'row'=16,'col'=16] {'row'}, use_global_device_ids=true, to_apply=%region_7.8 | all-reduce | flops 256 | bytes 2048 | tf_op jit(solution)/shard_map/psum | solution.py:68
  660.6 0.7 fusion.24
  661.4 176.6 %all-gather.9.cloned.1.call-done = bf16[2,2,2048,128]{3,2,0,1:T(8,128)(2,1)} async-done(((bf16[2,2,128,128]{3,2,0,1:T(8,128)(2,1)}), bf16[2,2,2048,128]{3,2,0,1:T(8,128)(2,1)}) %all-gather.9.cloned.1.call-update) | async-done | bytes 2097168 | tf_op jit(solution)/shard_map/all_gather | solution.py:56
  837.9 1.8 fusion.12
  840.7 0.5 add_reduce_fusion.1
  841.2 30.9 %psum.53 = f32[2,128]{1,0:T(2,128)S(1)} all-reduce(f32[2,128]{1,0:T(2,128)S(1)} %get-tuple-element.15), channel_id=1, replica_groups=mesh['bin'=2,'row'=16,'col'=16] {'row'}, use_global_device_ids=true, to_apply=%region_9.10 | all-reduce | flops 256 | bytes 2048 | tf_op jit(solution)/shard_map/psum | solution.py:28
  872.2 28.5 %psum.54 = f32[2,128]{1,0:T(2,128)S(1)} all-reduce(f32[2,128]{1,0:T(2,128)S(1)} %fusion.20), channel_id=1, replica_groups=mesh['bin'=2,'row'=16,'col'=16] {'row'}, use_global_device_ids=true, to_apply=%region_11.12 | all-reduce | flops 256 | bytes 2048 | tf_op jit(solution)/shard_map/psum | solution.py:68
  900.7 0.8 fusion.23
  901.5 72.5 %all-gather.11.cloned.1.call-done = bf16[2,2,2048,128]{3,2,0,1:T(8,128)(2,1)} async-done(((bf16[2,2,128,128]{3,2,0,1:T(8,128)(2,1)}), bf16[2,2,2048,128]{3,2,0,1:T(8,128)(2,1)}) %all-gather.11.cloned.1.call-update) | async-done | bytes 2097168 | tf_op jit(solution)/shard_map/all_gather | solution.py:56
  974.0 1.8 fusion.14
  976.8 1.1 copy-done.2
  978.4 30.9 %psum.55 = f32[2,128]{1,0:T(2,128)S(1)} all-reduce(f32[2,128]{1,0:T(2,128)S(1)} %get-tuple-element.17), channel_id=1, replica_groups=mesh['bin'=2,'row'=16,'col'=16] {'row'}, use_global_device_ids=true, to_apply=%region_13.14 | all-reduce | flops 256 | bytes 2048 | tf_op jit(solution)/shard_map/psum | solution.py:28
  1009.4 0.7 copy.12
  1010.2 0.7 copy.13
  (41 shorter events, 3.8 us)
Async XLA Ops:
  7.2 589.7 %all-gather.7.cloned.1.call-start = ((), (), s32[]{:S(2)}) async-start(), calls=%async_computation.1 | async-start | bytes 2228224 | tf_op jit(solution)/shard_map/all_gather | solution.py:56
  8.9 588.0 %all-gather.5.cloned.1.call-start = ((), (), s32[]{:S(2)}) async-start(), calls=%async_computation | async-start | bytes 2228224 | tf_op jit(solution)/shard_map/all_gather | solution.py:48
  10.5 827.4 %all-gather.9.cloned.1.call-start = ((), (), s32[]{:S(2)}) async-start(), calls=%async_computation.2 | async-start | bytes 2228224 | tf_op jit(solution)/shard_map/all_gather | solution.py:56
  596.9 2.2 copy-start.1
  599.1 1.8 copy-start
  599.1 2.0 copy-start.3
  661.3 312.7 %all-gather.11.cloned.1.call-start = ((), (), s32[]{:S(2)}) async-start(), calls=%async_computation.3 | async-start | bytes 2228224 | tf_op jit(solution)/shard_map/all_gather | solution.py:56
  837.9 1.9 copy-start.4
  974.0 1.9 copy-start.5
  976.3 1.6 copy-start.2
Sparse Core Ops, SparseCore 0:
  11.6 63.5 all-gather.6
  77.7 69.2 all-gather.4
  661.4 176.4 all-gather.8
  901.6 72.2 all-gather.10
where the time goes:
time: 1030 us; the launch traced here: 1020 us
  blocking collectives  729 us (71%)
  waiting for transfers between devices  249 us (24%)
  between operations  13.9 us (1%)
  local copies, waits for them, and re-layouts  12.4 us (1%)
  matrix products  11.1 us (1%)
    psum x1, blocking collectives, local(): trace_total = lax.psum(local_trace, ('row', 'col'))  580 us
    all_gather x3, waiting for transfers between devices, local(): piece = lax.all_gather(lowered, 'row', axis=2, tiled=True)  249 us
    psum x2, blocking collectives, curvature_sum(): return lax.psum(column_sum(direction, image), 'row')  61.8 us
    psum x2, blocking collectives, local(): norm_next = lax.psum(column_sum(residual, residual), 'row')  58.5 us
    psum x1, blocking collectives, local(): norm_now = lax.psum(column_sum(residual, residual), 'row')  28.5 us
  transfers between devices with their start and end apart: 4, of which 2 were waited for; matrix products, arithmetic and copies ran while one was open for 1% of the time, Pallas kernels for 0%

commit v1 on v0

v1 whole, which is shorter than its diff:
```python
import jax
import jax.numpy as jnp
from jax import lax
from jax.experimental import pallas as pl
from jax.experimental.pallas import tpu as pltpu
from jax.sharding import PartitionSpec as P

MESH = pl.DeviceIdType.MESH
N = 2048
ITERS = 3
EPS_REL = 0.1
T = 128
SB = 8
LANES = 512


def kernel(gamma, rhs, out_s, out_r,
           W, bT, B, X, Xs, Y, Z, shs, dir_, res, sol, img, O, R,
           zr, zs, br, bs, rs, ss, xr, xs, yr, ys, shr_sem, shs_sem, orr, ors):
    h = lax.axis_index("bin")
    i = lax.axis_index("row")
    z = lax.axis_index("col")
    y, x = i // 4, i % 4
    j = z // 4
    hb, bl_me = (z % 4) // 2, z % 2
    big = i // 2
    first_half = y < 2

    def dev(b, r, c):
        return {"bin": b, "row": r, "col": c}

    def is_me(b, r, c):
        return (b == h) & (r == i) & (c == z)

    def step_x(row, d):
        return (row // 4) * 4 + (row % 4 + d) % 4

    def step_y(row, d):
        return (row // 4 + d) % 4 * 4 + row % 4

    barrier = pltpu.get_barrier_semaphore()

    def greet(b, r, c, maybe_me):
        def far():
            pl.semaphore_signal(barrier, inc=1, device_id=dev(b, r, c), device_id_type=MESH)
        if maybe_me:
            pl.when(jnp.logical_not(is_me(b, r, c)))(far)
        else:
            far()

    for k in range(16):
        greet(hb, i, k, True)
    for k in range(16):
        greet(hb, k, 4 * j + x, True)
    for d in (1, 2, 3):
        greet(h, step_x(i, d), z, False)
        greet(h, step_y(i, d), z, False)
    greet(1 - h, i, z, False)

    for bl in range(2):
        for part in range(2):
            tile = rhs[bl, part].T
            for g in range(8):
                bT[bl, g, 16 * part:16 * part + 16, :] = tile[16 * g:16 * g + 16, :]

    mine = jnp.where(h == hb, 1, 0)
    pl.semaphore_wait(barrier, 39 - mine - mine * jnp.where(z % 4 == x, 1, 0))

    def send(src, dst, send_sem, recv_sem, target):
        return pltpu.make_async_remote_copy(
            src_ref=src, dst_ref=dst, send_sem=send_sem, recv_sem=recv_sem,
            device_id=dev(*target), device_id_type=MESH)

    t = (z - 2 * big + 16) % 16
    chosen = (t < 8) | ((t < 10) & (big < 4))

    def tile_copies():
        n = 0
        for bl in range(2):
            for jj in range(4):
                for q in range(2):
                    target = (q, i, 4 * jj + 2 * h + bl)
                    yield is_me(*target), target, gamma.at[bl, q], zs.at[n]
                    n += 1

    @pl.when(chosen)
    def _():
        for me, target, src, sem in tile_copies():
            @pl.when(jnp.logical_not(me))
            def _(src=src, sem=sem, target=target):
                send(src, W.at[i, t], sem, zr.at[t], target).start()
            @pl.when(me)
            def _(src=src):
                pltpu.make_async_copy(src, W.at[i, t], zr.at[t]).start()

    def rhs_copies():
        n = 0
        for bl in range(2):
            for yy in range(4):
                for q in range(2):
                    target = (q, 4 * yy + z % 4, 4 * j + 2 * h + bl)
                    yield is_me(*target), target, bT.at[bl, 2 * yy + q], bs.at[n], B.at[i]
                    n += 1

    for me, target, src, sem, dst in rhs_copies():
        @pl.when(jnp.logical_not(me))
        def _(src=src, sem=sem, dst=dst, target=target):
            send(src, dst, sem, br.at[i], target).start()
        @pl.when(me)
        def _(src=src, dst=dst):
            pltpu.make_async_copy(src, dst, br.at[i]).start()

    sib = (1 - h, i, z)

    def panel(row, d):
        return W.at[row, 2 * d:2 * d + 2]

    def panel_send(row, d, n, target_row):
        return send(panel(row, d), panel(row, d), ss.at[d, n], rs.at[row, d], (h, target_row, z))

    def panel_wait(row, d):
        panel_send(row, d, 0, step_x(i, 1)).wait_recv()

    def axes(d):
        return (step_x, step_y) if d % 2 == 0 else (step_y, step_x)

    def when(cond, body):
        if cond is True:
            body()
        else:
            pl.when(cond)(body)

    def row_ok(d, row):
        return True if d < 4 else row < 8

    def forward_side(d, e):
        return 1 if (d // 2 + e) % 2 == 0 else 3

    def stage_a(d):
        first, second = axes(d)
        def body():
            for u in (2 * d, 2 * d + 1):
                send(gamma.at[0, 0], W.at[i, u], zs.at[0], zr.at[u], sib).wait_recv()
            for n, e in enumerate((1, 3, 2)):
                panel_send(i, d, n, first(i, e)).start()
            for n, e in enumerate((1, 3)):
                panel_send(i, d, 3 + n, second(i, e)).start()
        when(row_ok(d, i), body)

    def stage_b(d):
        first, second = axes(d)
        def body():
            for n, e in enumerate((1, 3, 2)):
                row = first(i, e)
                panel_wait(row, d)
                for m, f in enumerate((1, 3)):
                    panel_send(row, d, 5 + 2 * n + m, second(i, f)).start()
        when(row_ok(d, i), body)

    def stage_c(d):
        first, second = axes(d)
        for side in (1, 3):
            def body(side=side):
                for e in range(4):
                    row = first(second(i, side), e)
                    panel_wait(row, d)
                    if forward_side(d, e) == side:
                        panel_send(row, d, 11 + e, second(i, 4 - side)).start()
            when(row_ok(d, second(i, side)), body)

    def stage_e(d):
        first, second = axes(d)
        def body():
            for e in range(4):
                panel_wait(first(second(i, 2), e), d)
        when(row_ok(d, second(i, 2)), body)

    def rhs_arrived():
        for k in range(16):
            send(bT.at[0, 0], B.at[k], bs.at[0], br.at[k], sib).wait_recv()
        for k in range(16):
            cols = slice(T * k, T * k + T)
            value = B[k]
            X[0, h, k] = value.astype(jnp.bfloat16)
            dir_[:, cols] = value
            res[:, cols] = value
        send(X.at[0, h], X.at[0, h], xs.at[0], xr.at[0], sib).start()
        sol[...] = jnp.zeros_like(sol)

    stage_a(0)
    stage_a(1)
    stage_b(0)
    stage_a(2)
    stage_b(1)
    stage_c(0)
    rhs_arrived()
    stage_a(3)
    stage_b(2)
    stage_c(1)
    stage_a(4)
    stage_b(3)
    stage_c(2)
    stage_b(4)
    stage_c(3)
    stage_c(4)
    for d in range(5):
        stage_e(d)

    total = jnp.zeros((T, T), jnp.float32)
    for k in range(16):
        total = total + W[k, k % 2].astype(jnp.float32)
    eye = lax.broadcasted_iota(jnp.int32, (T, T), 0) == lax.broadcasted_iota(jnp.int32, (T, T), 1)
    total = jnp.where(eye, total, 0.0)
    trace = jnp.sum(jnp.sum(total, axis=0, keepdims=True), axis=1, keepdims=True)
    shs[0] = jnp.broadcast_to(EPS_REL * trace / N, (8, T))
    shift_copy = send(shs.at[0], shs.at[1], shs_sem.at[0], shr_sem.at[0], sib)
    shift_copy.start()

    def both(v):
        s = v[:16] + v[16:]
        return jnp.concatenate([s, s], axis=0)

    def row_sum(parts):
        total = parts[0]
        for p in parts[1:]:
            total = total + p
        return both(jnp.sum(total, axis=1, keepdims=True))

    slabs = [slice(a, a + LANES) for a in range(0, N, LANES)]
    rr0 = row_sum([res[:, s] * res[:, s] for s in slabs])
    shift_copy.wait()
    shift = jnp.where(h == 0, shs[0], shs[1])[:1, :1]

    sign = jnp.where(h == 0, 1.0, -1.0).astype(jnp.bfloat16)

    def super_tile(a, d):
        return jnp.concatenate(
            [jnp.concatenate([W[2 * a, 2 * d], W[2 * a, 2 * d + 1]], axis=1),
             jnp.concatenate([W[2 * a + 1, 2 * d], W[2 * a + 1, 2 * d + 1]], axis=1)], axis=0)

    def x_block(ref_value, a):
        return jnp.concatenate([ref_value(2 * a), ref_value(2 * a + 1)], axis=1)

    def iteration(it, rr):
        send(X.at[it, h], X.at[it, h], xs.at[it], xr.at[it], sib).wait_recv()
        for k in range(16):
            Xs[k] = X[it, :, k].reshape(64, T) * sign

        def plain(k):
            return X[it, :, k].reshape(64, T)

        def signed(k):
            return Xs[k]

        for c in range(SB):
            acc = jnp.zeros((64, 256), jnp.float32)
            for d in range(5):
                a = (c - d) % SB
                if d < 4 or a < 4:
                    acc = acc + jnp.dot(x_block(signed, a), super_tile(a, d), preferred_element_type=jnp.float32)
                if d > 0 and (d < 4 or c < 4):
                    k = (c + d) % SB
                    acc = acc + lax.dot_general(
                        x_block(plain, k), super_tile(c, d), (((1,), (1,)), ((), ())),
                        preferred_element_type=jnp.float32)
            Y[:, :, 256 * c:256 * c + 256] = acc.reshape(2, 32, 256)

        swap = send(Y.at[1 - h], Z.at[it], ys.at[it], yr.at[it], sib)
        swap.start()
        swap.wait()

        curve = []
        for s in slabs:
            own, other = Y[h, :, s], Z[it, :, s]
            real = jnp.where(h == 0, own, other)
            imag = jnp.where(h == 0, other, own)
            d = dir_[:, s]
            image = real + jnp.concatenate([-imag[16:], imag[:16]], axis=0) + shift * d
            img[:, s] = image
            curve.append(d * image)
        alpha = rr / row_sum(curve)
        norm = []
        for s in slabs:
            sol[:, s] = sol[:, s] + alpha * dir_[:, s]
            r = res[:, s] - alpha * img[:, s]
            res[:, s] = r
            norm.append(r * r)
        new = row_sum(norm)

        @pl.when(it + 1 < ITERS)
        def _():
            beta = new / rr
            for k in range(16):
                cols = slice(T * k, T * k + T)
                d = res[:, cols] + beta * dir_[:, cols]
                dir_[:, cols] = d
                X[it + 1, h, k] = d.astype(jnp.bfloat16)
            send(X.at[it + 1, h], X.at[it + 1, h], xs.at[it + 1], xr.at[it + 1], sib).start()

        return new

    lax.fori_loop(0, ITERS, iteration, rr0)

    for k in range(16):
        cols = slice(T * k, T * k + T)
        O[k, 0] = sol[:, cols].astype(jnp.bfloat16)
        O[k, 1] = res[:, cols].astype(jnp.bfloat16)

    def out_copies():
        for k in range(16):
            target = (hb, k, 4 * j + x)
            yield is_me(*target), target, O.at[k], ors.at[k]

    dst, arrive = R.at[bl_me, 2 * y + h], orr.at[bl_me, 2 * y + h]
    for me, target, src, sem in out_copies():
        @pl.when(jnp.logical_not(me))
        def _(src=src, sem=sem, target=target):
            send(src, dst, sem, arrive, target).start()
        @pl.when(me)
        def _(src=src):
            pltpu.make_async_copy(src, dst, arrive).start()

    for bl in range(2):
        for g in range(8):
            send(O.at[0], R.at[bl, g], ors.at[0], orr.at[bl, g], sib).wait_recv()
        for n, out in enumerate((out_s, out_r)):
            for part in range(2):
                tile = jnp.concatenate(
                    [R[bl, g, n, 16 * part:16 * part + 16, :].astype(jnp.float32) for g in range(8)], axis=0)
                out[bl, part] = tile.T

    @pl.when(chosen)
    def _():
        for me, target, src, sem in tile_copies():
            @pl.when(jnp.logical_not(me))
            def _(src=src, sem=sem, target=target):
                send(src, W.at[i, t], sem, zr.at[t], target).wait_send()
    for me, target, src, sem, to in rhs_copies():
        @pl.when(jnp.logical_not(me))
        def _(src=src, sem=sem, to=to, target=target):
            send(src, to, sem, br.at[i], target).wait_send()
    for me, target, src, sem in out_copies():
        @pl.when(jnp.logical_not(me))
        def _(src=src, sem=sem, target=target):
            send(src, dst, sem, arrive, target).wait_send()
    for d in range(5):
        first, second = axes(d)
        def own(d=d):
            for n in range(11):
                panel_send(i, d, n, step_x(i, 1)).wait_send()
        when(row_ok(d, i), own)
        for e in range(4):
            def passed(d=d, e=e):
                panel_send(i, d, 11 + e, step_x(i, 1)).wait_send()
            when(row_ok(d, second(i, forward_side(d, e))), passed)
    for it in range(ITERS):
        send(X.at[it, h], X.at[it, h], xs.at[it], xr.at[it], sib).wait_send()


def local(gamma, rhs):
    vmem = pl.BlockSpec(memory_space=pltpu.VMEM)
    dma = pltpu.SemaphoreType.DMA
    f32, bf16 = jnp.float32, jnp.bfloat16
    shape = jax.ShapeDtypeStruct(rhs.shape, f32)
    return pl.pallas_call(
        kernel,
        out_shape=(shape, shape),
        in_specs=[vmem, vmem],
        out_specs=(vmem, vmem),
        scratch_shapes=[
            pltpu.VMEM((16, 10, T, T), bf16),
            pltpu.VMEM((2, 8, 32, T), f32),
            pltpu.VMEM((16, 32, T), f32),
            pltpu.VMEM((ITERS, 2, 16, 32, T), bf16),
            pltpu.VMEM((16, 64, T), bf16),
            pltpu.VMEM((2, 32, N), f32),
            pltpu.VMEM((ITERS, 32, N), f32),
            pltpu.VMEM((2, 8, T), f32),
            pltpu.VMEM((32, N), f32),
            pltpu.VMEM((32, N), f32),
            pltpu.VMEM((32, N), f32),
            pltpu.VMEM((32, N), f32),
            pltpu.VMEM((16, 2, 32, T), bf16),
            pltpu.VMEM((2, 8, 2, 32, T), bf16),
            dma((10,)), dma((16,)), dma((16,)), dma((16,)), dma((16, 5)), dma((5, 15)),
            dma((ITERS,)), dma((ITERS,)), dma((ITERS,)), dma((ITERS,)), dma((1,)), dma((1,)),
            dma((2, 8)), dma((16,)),
        ],
        compiler_params=pltpu.CompilerParams(
            collective_id=0, has_side_effects=True, vmem_limit_bytes=40 * 2**20),
    )(gamma, rhs)


def solution(mesh):
    spec = P("bin", None, "row", "col")
    return jax.shard_map(local, mesh=mesh, in_specs=(spec, spec), out_specs=(spec, spec), check_vma=False)
```

time: 1030 us -> 106 us (0.10)
  the two profiles are of different devices: /device:TPU:33 before, /device:TPU:30 now
where the time goes in v1:
time: 106 us
  Pallas kernels  102 us (96%)
  local copies, waits for them, and re-layouts  3.25 us (3%)
    pallas_call x1, Pallas kernels, local(): pl.pallas_call(kernel, out_shape=(shape, shape), in_specs=[vmem, vmem], o...  102 us
    unnamed x6, local copies, waits for them, and re-layouts  3.25 us

profile of v1, /device:TPU:30, one launch (start us, length us, event | category | flops | bytes accessed | tf_op | source)
XLA Modules:
  0.0 106.0 jit_solution(1039900673423639914)
XLA Ops:
  0.6 0.0 copy-start
  0.6 0.9 copy-done
  1.6 0.0 copy-start.1
  1.6 0.9 copy-done.1
  2.5 102.1 %shard_map.41 = (f32[2,2,128,128]{3,2,1,0:T(8,128)S(1)}, f32[2,2,128,128]{3,2,1,0:T(8,128)S(1)}) custom-call(bf16[2,2,128,128]{3,2,1,0:T(8,128)(2,1)S(1)} %copy-done.1, f32[2,2,128,128]{3,2,1,0:T(8,128)S(1)} %copy-done), custom_call_target="tpu_custom_call" | custom-call | tf_op jit(solution)/shard_map/pallas_call | solution.py:365
  104.6 0.7 copy.6
  105.3 0.7 copy.7
Async XLA Ops:
  0.6 1.0 copy-start
  1.6 0.9 copy-start.1

commit v2 on v1

v2 whole, which is shorter than its diff:
```python
import jax
import jax.numpy as jnp
from jax import lax
from jax.experimental import pallas as pl
from jax.experimental.pallas import tpu as pltpu
from jax.sharding import PartitionSpec as P

MESH = pl.DeviceIdType.MESH
N = 2048
ITERS = 3
EPS_REL = 0.1
T = 128
SB = 8
APART = (0, 3, 6, 1, 4)
CHUNKS = ((0, 2), (2, 4), (4, 6), (6, 8), (8, 9), (9, 10))


def kernel(gamma, rhs, out_s, out_r,
           W, tile_in, bT, B, X, Xs, Y, Z, shs, dir_, res, sol, img, O, R,
           zr, zs, ws, br, bs, rs, ss, xr, xs, yr, ys, shr_sem, shs_sem, orr, ors, in_sem):
    h = lax.axis_index("bin")
    i = lax.axis_index("row")
    z = lax.axis_index("col")
    y, x = i // 4, i % 4
    hb, bl_me = (z % 4) // 2, z % 2
    big = i // 2
    home = (z + 17 - x) % 16

    fetch = pltpu.make_async_copy(rhs, tile_in, in_sem.at[0])
    fetch.start()

    def dev(b, r, c):
        return {"bin": b, "row": r, "col": c}

    def is_me(b, r, c):
        return (b == h) & (r == i) & (c == z)

    def step_x(row, d):
        return (row // 4) * 4 + (row % 4 + d) % 4

    def step_y(row, d):
        return (row // 4 + d) % 4 * 4 + row % 4

    def step_z(d):
        return (z + d + 16) % 16

    barrier = pltpu.get_barrier_semaphore()

    def greet(b, r, c, maybe_me):
        def far():
            pl.semaphore_signal(barrier, inc=1, device_id=dev(b, r, c), device_id_type=MESH)
        if maybe_me:
            pl.when(jnp.logical_not(is_me(b, r, c)))(far)
        else:
            far()

    for d in (4, -4):
        greet(hb, i, step_z(d), False)
        greet(h, i, step_z(d), False)
    for d in (3, -3, 2, -2, 1, -1):
        greet(hb, i, step_z(d), False)
    greet(hb, i, z, True)
    for k in range(16):
        greet(hb, k, home, True)
    for d in (1, 2, 3):
        greet(h, step_x(i, d), z, False)
        greet(h, step_y(i, d), z, False)
    greet(1 - h, i, z, False)

    fetch.wait()
    for bl in range(2):
        for part in range(2):
            tile = tile_in[bl, part].T
            for g in range(8):
                bT[bl, g, 16 * part:16 * part + 16, :] = tile[16 * g:16 * g + 16, :]

    mine = jnp.where(h == hb, 1, 0)
    pl.semaphore_wait(barrier, 33 + mine - mine * jnp.where(x == 1, 1, 0))

    def send(src, dst, send_sem, recv_sem, target):
        return pltpu.make_async_remote_copy(
            src_ref=src, dst_ref=dst, send_sem=send_sem, recv_sem=recv_sem,
            device_id=dev(*target), device_id_type=MESH)

    sib = (1 - h, i, z)

    apart = (z // 2 - big + 8) % 8
    slot = jnp.where(apart == 0, 0, jnp.where(apart == 3, 1, jnp.where(apart == 6, 2, jnp.where(apart == 1, 3, 4))))
    chosen = (slot < 4) | ((apart == 4) & (big < 4))
    t = 2 * slot + z % 2

    def tile_copies():
        n = 0
        for bl in range(2):
            ahead = (2 * h + bl + 4 - z % 4) % 4
            for q in range(2):
                for kind in range(3):
                    if kind == 0:
                        target, cond = (q, i, step_z(ahead)), jnp.logical_not((ahead == 0) & (q == h))
                    elif kind == 1:
                        target, cond = (q, i, step_z(ahead - 4)), True
                    else:
                        target, cond = (q, i, step_z(4)), ahead == 0
                    yield cond, target, gamma.at[bl, q], zs.at[n]
                    n += 1

    def when(cond, body):
        if cond is True:
            body()
        else:
            pl.when(cond)(body)

    def send_tiles():
        for cond, target, src, sem in tile_copies():
            when(cond, lambda: send(src, W.at[i, t], sem, zr.at[t], target).start())
        @pl.when(h == hb)
        def _():
            pltpu.make_async_copy(gamma.at[bl_me, h], W.at[i, t], zr.at[t]).start()

    def tile_wait(u):
        send(gamma.at[0, 0], W.at[i, u], zs.at[0], zr.at[u], sib).wait_recv()

    def route(u):
        off = (z - 2 * (big + APART[u // 2]) - u % 2 + 32) % 16
        up = ((off >= 1) & (off <= 3)) | ((off == 4) & (h == 0))
        down = (off >= 13) | ((off == 12) & (h == 1))
        near = (off <= 4) | (off >= 12)
        return near, up | down, (h, i, step_z(jnp.where(up, 4, -4)))

    def tile_pass(u, target):
        return send(W.at[i, u], W.at[i, u], ws.at[u], zr.at[u], target)

    def slot_ok(u, row):
        return True if u < 8 else row < 8

    def both_conds(a, b):
        return a if b is True else a & b

    def near_tiles(slots):
        for u in slots:
            near, relay, target = route(u)
            @pl.when(both_conds(near, slot_ok(u, i)))
            def _(u=u, relay=relay, target=target):
                tile_wait(u)
                @pl.when(relay)
                def _():
                    tile_pass(u, target).start()

    def far_tiles(slots):
        for u in slots:
            near, _, _ = route(u)
            @pl.when(both_conds(jnp.logical_not(near), slot_ok(u, i)))
            def _(u=u):
                tile_wait(u)

    def rhs_copies():
        n = 0
        for bl in range(2):
            xx = (2 * h + bl + 5 - z % 4) % 4
            for yy in range(4):
                for q in range(2):
                    target = (q, 4 * yy + xx, (z + 15 + xx) % 16)
                    yield is_me(*target), target, bT.at[bl, 2 * yy + q], bs.at[n]
                    n += 1

    def send_rhs():
        for me, target, src, sem in rhs_copies():
            pl.when(jnp.logical_not(me))(lambda: send(src, B.at[i], sem, br.at[i], target).start())
            pl.when(me)(lambda: pltpu.make_async_copy(src, B.at[i], br.at[i]).start())

    def panel(row, c):
        a, b = CHUNKS[c]
        return W.at[row, a:b]

    def panel_send(row, c, n, target_row):
        return send(panel(row, c), panel(row, c), ss.at[c, n], rs.at[row, c], (h, target_row, z))

    def panel_wait(row, c):
        panel_send(row, c, 0, step_x(i, 1)).wait_recv()

    def axes(c):
        return (step_x, step_y) if c % 2 == 0 else (step_y, step_x)

    def row_ok(c, row):
        return True if c < 4 else row < 8

    def forward_side(c, e):
        return 1 if (c // 2 + e) % 2 == 0 else 3

    def stage_a(c):
        first, second = axes(c)
        def body():
            for n, e in enumerate((1, 3, 2)):
                panel_send(i, c, n, first(i, e)).start()
            for n, e in enumerate((1, 3)):
                panel_send(i, c, 3 + n, second(i, e)).start()
        when(row_ok(c, i), body)

    def stage_b(c):
        first, second = axes(c)
        for n, e in enumerate((1, 3, 2)):
            row = first(i, e)
            def body(n=n, row=row):
                panel_wait(row, c)
                for m, f in enumerate((1, 3)):
                    panel_send(row, c, 5 + 2 * n + m, second(i, f)).start()
            when(row_ok(c, row), body)

    def stage_c(c):
        first, second = axes(c)
        for side in (1, 3):
            for e in range(4):
                row = first(second(i, side), e)
                def body(side=side, e=e, row=row):
                    panel_wait(row, c)
                    if forward_side(c, e) == side:
                        panel_send(row, c, 11 + e, second(i, 4 - side)).start()
                when(row_ok(c, row), body)

    def stage_e(c):
        first, second = axes(c)
        for e in range(4):
            row = first(second(i, 2), e)
            when(row_ok(c, row), lambda: panel_wait(row, c))

    def x_copy(it):
        return send(X.at[it, h], X.at[it, h], xs.at[it], xr.at[it], sib)

    sign = jnp.where(h == 0, 1.0, -1.0).astype(jnp.bfloat16)

    def x_ready(it):
        x_copy(it).wait_recv()
        for k in range(16):
            Xs[k] = X[it, :, k].reshape(64, T) * sign

    def rhs_arrived():
        for k in range(16):
            send(bT.at[0, 0], B.at[k], bs.at[0], br.at[k], sib).wait_recv()
            X[0, h, k] = B[k].astype(jnp.bfloat16)
        x_copy(0).start()
        for k in range(16):
            cols = slice(T * k, T * k + T)
            dir_[:, cols] = B[k]
            res[:, cols] = B[k]
        sol[...] = jnp.zeros_like(sol)

    def super_tile(a, n):
        return jnp.concatenate(
            [jnp.concatenate([W[2 * a, 2 * n], W[2 * a, 2 * n + 1]], axis=1),
             jnp.concatenate([W[2 * a + 1, 2 * n], W[2 * a + 1, 2 * n + 1]], axis=1)], axis=0)

    def products(it, c, n, acc):
        def add(acc, v):
            return v if acc is None else acc + v
        d = APART[n]
        a = (c - d) % SB
        if n < 4 or a < 4:
            left = jnp.concatenate([Xs[2 * a], Xs[2 * a + 1]], axis=1)
            acc = add(acc, jnp.dot(left, super_tile(a, n), preferred_element_type=jnp.float32))
        k = (c + d) % SB
        if n > 0 and (n < 4 or c < 4):
            left = jnp.concatenate([X[it, :, 2 * k].reshape(64, T), X[it, :, 2 * k + 1].reshape(64, T)], axis=1)
            acc = add(acc, lax.dot_general(
                left, super_tile(c, n), (((1,), (1,)), ((), ())), preferred_element_type=jnp.float32))
        return acc

    def y_copy(it, c):
        return send(Y.at[1 - h, c], Z.at[it, c], ys.at[it, c], yr.at[it, c], sib)

    def first_product(n):
        for c in range(SB):
            acc = products(0, c, n, None if n == 0 else Y[:, c].reshape(64, 256))
            Y[:, c] = acc.reshape(2, 32, 256)
            if n == 4:
                y_copy(0, c).start()

    first_slots, later_slots = range(4), range(4, 10)

    pl.when(chosen & (slot < 2))(send_tiles)
    send_rhs()
    near_tiles(first_slots)
    far_tiles((0, 1))
    stage_a(0)
    far_tiles((2, 3))
    stage_a(1)
    pl.when(chosen & (slot >= 2))(send_tiles)
    stage_b(0)
    stage_b(1)
    rhs_arrived()
    near_tiles(later_slots)
    stage_c(0)
    far_tiles((4, 5))
    stage_a(2)
    far_tiles((6, 7))
    stage_a(3)
    far_tiles((8, 9))
    stage_a(4)
    stage_a(5)
    stage_c(1)
    for c in range(2, 6):
        stage_b(c)
    stage_e(0)
    x_ready(0)
    first_product(0)
    stage_e(1)
    stage_c(2)
    stage_c(3)
    first_product(1)

    total = jnp.zeros((T, T), jnp.float32)
    for k in range(16):
        total = total + W[k, k % 2].astype(jnp.float32)
    eye = lax.broadcasted_iota(jnp.int32, (T, T), 0) == lax.broadcasted_iota(jnp.int32, (T, T), 1)
    total = jnp.where(eye, total, 0.0)
    trace = jnp.sum(jnp.sum(total, axis=0, keepdims=True), axis=1, keepdims=True)
    shs[0] = jnp.broadcast_to(EPS_REL * trace / N, (8, T))
    shift_copy = send(shs.at[0], shs.at[1], shs_sem.at[0], shr_sem.at[0], sib)
    shift_copy.start()

    stage_c(4)
    stage_c(5)
    stage_e(2)
    first_product(2)
    stage_e(3)
    first_product(3)
    stage_e(4)
    stage_e(5)
    first_product(4)

    def both(v):
        s = v[:16] + v[16:]
        return jnp.concatenate([s, s], axis=0)

    def row_sum(parts):
        total = parts[0]
        for p in parts[1:]:
            total = total + p
        return both(jnp.sum(total, axis=1, keepdims=True))

    slabs = [slice(256 * c, 256 * c + 256) for c in range(SB)]
    rr0 = row_sum([res[:, s] * res[:, s] for s in slabs])
    shift_copy.wait()
    shift = jnp.where(h == 0, shs[0], shs[1])[:1, :1]

    def iteration(it, rr):
        curve = []
        for c, s in enumerate(slabs):
            y_copy(it, c).wait()
            own, other = Y[h, c], Z[it, c]
            real = jnp.where(h == 0, own, other)
            imag = jnp.where(h == 0, other, own)
            d = dir_[:, s]
            image = real + jnp.concatenate([-imag[16:], imag[:16]], axis=0) + shift * d
            img[:, s] = image
            curve.append(d * image)
        alpha = rr / row_sum(curve)
        norm = []
        for s in slabs:
            sol[:, s] = sol[:, s] + alpha * dir_[:, s]
            r = res[:, s] - alpha * img[:, s]
            res[:, s] = r
            norm.append(r * r)
        new = row_sum(norm)

        @pl.when(it + 1 < ITERS)
        def _():
            beta = new / rr
            for k in range(16):
                cols = slice(T * k, T * k + T)
                d = res[:, cols] + beta * dir_[:, cols]
                dir_[:, cols] = d
                X[it + 1, h, k] = d.astype(jnp.bfloat16)
            x_copy(it + 1).start()
            x_ready(it + 1)
            for c in range(SB):
                acc = None
                for n in range(5):
                    acc = products(it + 1, c, n, acc)
                Y[:, c] = acc.reshape(2, 32, 256)
                y_copy(it + 1, c).start()

        return new

    lax.fori_loop(0, ITERS, iteration, rr0)

    dst, arrive = R.at[bl_me, 2 * y + h], orr.at[bl_me, 2 * y + h]

    def out_copies():
        for k in range(16):
            target = (hb, k, home)
            yield is_me(*target), target, O.at[k], ors.at[k], k

    for me, target, src, sem, k in out_copies():
        cols = slice(T * k, T * k + T)
        O[k, 0] = sol[:, cols].astype(jnp.bfloat16)
        O[k, 1] = res[:, cols].astype(jnp.bfloat16)
        pl.when(jnp.logical_not(me))(lambda: send(src, dst, sem, arrive, target).start())
        pl.when(me)(lambda: pltpu.make_async_copy(src, dst, arrive).start())

    for bl in range(2):
        for g in range(8):
            send(O.at[0], R.at[bl, g], ors.at[0], orr.at[bl, g], sib).wait_recv()
        for n, out in enumerate((out_s, out_r)):
            for part in range(2):
                tile = jnp.concatenate(
                    [R[bl, g, n, 16 * part:16 * part + 16, :].astype(jnp.float32) for g in range(8)], axis=0)
                out[bl, part] = tile.T

    @pl.when(chosen)
    def _():
        for cond, target, src, sem in tile_copies():
            when(cond, lambda: send(src, W.at[i, t], sem, zr.at[t], target).wait_send())
    for u in range(10):
        _, relay, target = route(u)
        pl.when(both_conds(relay, slot_ok(u, i)))(lambda: tile_pass(u, target).wait_send())
    for me, target, src, sem in rhs_copies():
        pl.when(jnp.logical_not(me))(lambda: send(src, B.at[i], sem, br.at[i], target).wait_send())
    for me, target, src, sem, k in out_copies():
        pl.when(jnp.logical_not(me))(lambda: send(src, dst, sem, arrive, target).wait_send())
    for c in range(6):
        first, second = axes(c)
        def own():
            for n in range(5):
                panel_send(i, c, n, step_x(i, 1)).wait_send()
        when(row_ok(c, i), own)
        for n, e in enumerate((1, 3, 2)):
            def peer():
                for m in range(2):
                    panel_send(i, c, 5 + 2 * n + m, step_x(i, 1)).wait_send()
            when(row_ok(c, first(i, e)), peer)
        for e in range(4):
            row = first(second(i, forward_side(c, e)), e)
            when(row_ok(c, row), lambda: panel_send(i, c, 11 + e, step_x(i, 1)).wait_send())
    for it in range(ITERS):
        x_copy(it).wait_send()


def local(gamma, rhs):
    vmem = pl.BlockSpec(memory_space=pltpu.VMEM)
    dma = pltpu.SemaphoreType.DMA
    f32, bf16 = jnp.float32, jnp.bfloat16
    shape = jax.ShapeDtypeStruct(rhs.shape, f32)
    return pl.pallas_call(
        kernel,
        out_shape=(shape, shape),
        in_specs=[pl.BlockSpec(memory_space=pl.ANY)] * 2,
        out_specs=(vmem, vmem),
        scratch_shapes=[
            pltpu.VMEM((16, 10, T, T), bf16),
            pltpu.VMEM((2, 2, T, T), f32),
            pltpu.VMEM((2, 8, 32, T), f32),
            pltpu.VMEM((16, 32, T), f32),
            pltpu.VMEM((ITERS, 2, 16, 32, T), bf16),
            pltpu.VMEM((16, 64, T), bf16),
            pltpu.VMEM((2, SB, 32, 256), f32),
            pltpu.VMEM((ITERS, SB, 32, 256), f32),
            pltpu.VMEM((2, 8, T), f32),
            pltpu.VMEM((32, N), f32),
            pltpu.VMEM((32, N), f32),
            pltpu.VMEM((32, N), f32),
            pltpu.VMEM((32, N), f32),
            pltpu.VMEM((16, 2, 32, T), bf16),
            pltpu.VMEM((2, 8, 2, 32, T), bf16),
            dma((10,)), dma((12,)), dma((10,)), dma((16,)), dma((16,)), dma((16, 6)), dma((6, 15)),
            dma((ITERS,)), dma((ITERS,)), dma((ITERS, SB)), dma((ITERS, SB)), dma((1,)), dma((1,)),
            dma((2, 8)), dma((16,)), dma((1,)),
        ],
        compiler_params=pltpu.CompilerParams(
            collective_id=0, has_side_effects=True, vmem_limit_bytes=60 * 2**20),
    )(gamma, rhs)


def solution(mesh):
    spec = P("bin", None, "row", "col")
    return jax.shard_map(local, mesh=mesh, in_specs=(spec, spec), out_specs=(spec, spec), check_vma=False)
```

time: 106 us -> 100 us (0.943)
  the two profiles are of different devices: /device:TPU:30 before, /device:TPU:57 now
where the time goes in v2:
time: 100 us; the launch traced here: 99.8 us
  Pallas kernels  96.7 us (97%)
  local copies, waits for them, and re-layouts  2.42 us (2%)
    pallas_call x1, Pallas kernels, local(): pl.pallas_call(kernel, out_shape=(shape, shape), in_specs=[pl.BlockSpec(m...  96.7 us
    unnamed x4, local copies, waits for them, and re-layouts  2.42 us

profile of v2, /device:TPU:57, one launch (start us, length us, event | category | flops | bytes accessed | tf_op | source)
XLA Modules:
  0.0 99.8 jit_solution(7887374969670018915)
XLA Ops:
  0.6 96.7 %shard_map.41 = (f32[2,2,128,128]{3,2,1,0:T(8,128)}, f32[2,2,128,128]{3,2,1,0:T(8,128)}) custom-call(bf16[2,2,128,128]{3,2,1,0:T(8,128)(2,1)} %gamma.1, f32[2,2,128,128]{3,2,1,0:T(8,128)} %rhs.1), custom_call_target="tpu_custom_call" | custom-call | tf_op jit(solution)/shard_map/pallas_call | solution.py:443
  97.4 0.0 copy-start
  97.4 1.7 %copy.6 = f32[2,2,128,128]{3,2,1,0:T(8,128)} copy(f32[2,2,128,128]{3,2,1,0:T(8,128)} %get-tuple-element.4) | data formatting | bytes 524288
  99.1 0.0 copy-done
  99.1 0.7 copy.7
Async XLA Ops:
  97.4 1.7 %copy-start = (f32[2,2,128,128]{3,2,1,0:T(8,128)S(1)}, f32[2,2,128,128]{3,2,1,0:T(8,128)}, u32[]{:S(2)}) copy-start(f32[2,2,128,128]{3,2,1,0:T(8,128)} %get-tuple-element.5) | copy-start | bytes 786436

commit v3 on v2

--- a/solution.py
+++ b/solution.py
@@ -11,13 +11,14 @@
 EPS_REL = 0.1
 T = 128
 SB = 8
+FAR_FIRST = ((2, 2), (2, 1), (2, 3), (1, 2), (3, 2), (1, 1), (1, 3), (3, 1), (3, 3), (2, 0), (0, 2), (1, 0), (3, 0), (0, 1), (0, 3), (0, 0))
 APART = (0, 3, 6, 1, 4)
 CHUNKS = ((0, 2), (2, 4), (4, 6), (6, 8), (8, 9), (9, 10))
 
 
-def kernel(gamma, rhs, out_s, out_r,
+def kernel(gamma, rhs, out,
            W, tile_in, bT, B, X, Xs, Y, Z, shs, dir_, res, sol, img, O, R,
-           zr, zs, ws, br, bs, rs, ss, xr, xs, yr, ys, shr_sem, shs_sem, orr, ors, in_sem):
+           zr, zs, ws, br, bs, rs, gs, ss, xr, xs, yr, ys, shr_sem, shs_sem, orr, ors, in_sem):
     h = lax.axis_index("bin")
     i = lax.axis_index("row")
     z = lax.axis_index("col")
@@ -66,13 +67,6 @@
         greet(h, step_x(i, d), z, False)
         greet(h, step_y(i, d), z, False)
     greet(1 - h, i, z, False)
-
-    fetch.wait()
-    for bl in range(2):
-        for part in range(2):
-            tile = tile_in[bl, part].T
-            for g in range(8):
-                bT[bl, g, 16 * part:16 * part + 16, :] = tile[16 * g:16 * g + 16, :]
 
     mine = jnp.where(h == hb, 1, 0)
     pl.semaphore_wait(barrier, 33 + mine - mine * jnp.where(x == 1, 1, 0))
@@ -112,13 +106,13 @@
 
     def send_tiles():
         for cond, target, src, sem in tile_copies():
-            when(cond, lambda: send(src, W.at[i, t], sem, zr.at[t], target).start())
+            when(cond, lambda: send(src, W.at[y, x, t], sem, zr.at[t], target).start())
         @pl.when(h == hb)
         def _():
-            pltpu.make_async_copy(gamma.at[bl_me, h], W.at[i, t], zr.at[t]).start()
+            pltpu.make_async_copy(gamma.at[bl_me, h], W.at[y, x, t], zr.at[t]).start()
 
     def tile_wait(u):
-        send(gamma.at[0, 0], W.at[i, u], zs.at[0], zr.at[u], sib).wait_recv()
+        send(gamma.at[0, 0], W.at[y, x, u], zs.at[0], zr.at[u], sib).wait_recv()
 
     def route(u):
         off = (z - 2 * (big + APART[u // 2]) - u % 2 + 32) % 16
@@ -128,7 +122,7 @@
         return near, up | down, (h, i, step_z(jnp.where(up, 4, -4)))
 
     def tile_pass(u, target):
-        return send(W.at[i, u], W.at[i, u], ws.at[u], zr.at[u], target)
+        return send(W.at[y, x, u], W.at[y, x, u], ws.at[u], zr.at[u], target)
 
     def slot_ok(u, row):
         return True if u < 8 else row < 8
@@ -153,6 +147,14 @@
             def _(u=u):
                 tile_wait(u)
 
+    def turn_rhs():
+        fetch.wait()
+        for bl in range(2):
+            for part in range(2):
+                tile = tile_in[bl, part].T
+                for g in range(8):
+                    bT[bl, g, 16 * part:16 * part + 16, :] = tile[16 * g:16 * g + 16, :]
+
     def rhs_copies():
         n = 0
         for bl in range(2):
@@ -168,60 +170,77 @@
             pl.when(jnp.logical_not(me))(lambda: send(src, B.at[i], sem, br.at[i], target).start())
             pl.when(me)(lambda: pltpu.make_async_copy(src, B.at[i], br.at[i]).start())
 
-    def panel(row, c):
+    def panel_send(row, c, n, target_row, part=None):
         a, b = CHUNKS[c]
-        return W.at[row, a:b]
-
-    def panel_send(row, c, n, target_row):
-        return send(panel(row, c), panel(row, c), ss.at[c, n], rs.at[row, c], (h, target_row, z))
-
-    def panel_wait(row, c):
-        panel_send(row, c, 0, step_x(i, 1)).wait_recv()
+        rows = slice(0, T) if part is None else slice(part * T // 2, (part + 1) * T // 2)
+        ref = W.at[row // 4, row % 4, a:b, rows]
+        arrive = rs.at[row, c, 0 if part is None else part]
+        return send(ref, ref, ss.at[c, n], arrive, (h, target_row, z))
+
+    def group_send(line, c, n, part, sem, target_row):
+        a, b = CHUNKS[c]
+        size = 2 if c == 5 else 4
+        lo, hi = (0, size) if part is None else (part * size // 2, (part + 1) * size // 2)
+        ref = W.at[line, lo:hi, a:b] if c % 2 == 0 else W.at[lo:hi, line, a:b]
+        return send(ref, ref, ss.at[c, n], gs.at[c, sem], (h, target_row, z))
 
     def axes(c):
         return (step_x, step_y) if c % 2 == 0 else (step_y, step_x)
 
+    def line_of(c, row):
+        return row // 4 if c % 2 == 0 else row % 4
+
     def row_ok(c, row):
         return True if c < 4 else row < 8
 
-    def forward_side(c, e):
-        return 1 if (c // 2 + e) % 2 == 0 else 3
+    def line_ok(c, line):
+        return line < 2 if c == 4 else True
 
     def stage_a(c):
-        first, second = axes(c)
+        first, _ = axes(c)
         def body():
-            for n, e in enumerate((1, 3, 2)):
+            for n, e in enumerate((1, 3)):
                 panel_send(i, c, n, first(i, e)).start()
-            for n, e in enumerate((1, 3)):
-                panel_send(i, c, 3 + n, second(i, e)).start()
         when(row_ok(c, i), body)
+
+    def stage_f(c):
+        first, _ = axes(c)
+        for e, part in ((1, 0), (3, 1)):
+            row = first(i, e)
+            def body():
+                panel_send(row, c, 0, first(i, 1)).wait_recv()
+                panel_send(row, c, 2 + 5 * part, first(i, 4 - e), part).start()
+            when(row_ok(c, row), body)
 
     def stage_b(c):
         first, second = axes(c)
-        for n, e in enumerate((1, 3, 2)):
-            row = first(i, e)
-            def body(n=n, row=row):
-                panel_wait(row, c)
-                for m, f in enumerate((1, 3)):
-                    panel_send(row, c, 5 + 2 * n + m, second(i, f)).start()
-            when(row_ok(c, row), body)
+        row = first(i, 2)
+        def halves():
+            for part in range(2):
+                panel_send(row, c, 0, first(i, 1), part).wait_recv()
+        when(row_ok(c, row), halves)
+        line = line_of(c, i)
+        def body():
+            group_send(line, c, 3, None, 1, second(i, 1)).start()
+            group_send(line, c, 4, None, 0, second(i, 3)).start()
+        when(line_ok(c, line), body)
 
     def stage_c(c):
-        first, second = axes(c)
-        for side in (1, 3):
-            for e in range(4):
-                row = first(second(i, side), e)
-                def body(side=side, e=e, row=row):
-                    panel_wait(row, c)
-                    if forward_side(c, e) == side:
-                        panel_send(row, c, 11 + e, second(i, 4 - side)).start()
-                when(row_ok(c, row), body)
+        _, second = axes(c)
+        for side, part in ((1, 0), (3, 1)):
+            line = line_of(c, second(i, side))
+            def body():
+                group_send(line, c, 3, None, part, second(i, 1)).wait_recv()
+                group_send(line, c, 5 + part, part, 2 + part, second(i, 4 - side)).start()
+            when(line_ok(c, line), body)
 
     def stage_e(c):
-        first, second = axes(c)
-        for e in range(4):
-            row = first(second(i, 2), e)
-            when(row_ok(c, row), lambda: panel_wait(row, c))
+        _, second = axes(c)
+        line = line_of(c, second(i, 2))
+        def body():
+            for part in range(2):
+                group_send(line, c, 3, part, 2 + part, second(i, 1)).wait_recv()
+        when(line_ok(c, line), body)
 
     def x_copy(it):
         return send(X.at[it, h], X.at[it, h], xs.at[it], xr.at[it], sib)
@@ -246,8 +265,8 @@
 
     def super_tile(a, n):
         return jnp.concatenate(
-            [jnp.concatenate([W[2 * a, 2 * n], W[2 * a, 2 * n + 1]], axis=1),
-             jnp.concatenate([W[2 * a + 1, 2 * n], W[2 * a + 1, 2 * n + 1]], axis=1)], axis=0)
+            [jnp.concatenate([W[a // 2, r, 2 * n], W[a // 2, r, 2 * n + 1]], axis=1)
+             for r in (2 * (a % 2), 2 * (a % 2) + 1)], axis=0)
 
     def products(it, c, n, acc):
         def add(acc, v):
@@ -264,52 +283,40 @@
                 left, super_tile(c, n), (((1,), (1,)), ((), ())), preferred_element_type=jnp.float32))
         return acc
 
-    def y_copy(it, c):
-        return send(Y.at[1 - h, c], Z.at[it, c], ys.at[it, c], yr.at[it, c], sib)
+    def y_copy(it):
+        return send(Y.at[1 - h], Z.at[it], ys.at[it], yr.at[it], sib)
 
     def first_product(n):
         for c in range(SB):
             acc = products(0, c, n, None if n == 0 else Y[:, c].reshape(64, 256))
             Y[:, c] = acc.reshape(2, 32, 256)
-            if n == 4:
-                y_copy(0, c).start()
-
-    first_slots, later_slots = range(4), range(4, 10)
-
-    pl.when(chosen & (slot < 2))(send_tiles)
+
+    pl.when(chosen)(send_tiles)
+    turn_rhs()
     send_rhs()
-    near_tiles(first_slots)
-    far_tiles((0, 1))
-    stage_a(0)
-    far_tiles((2, 3))
-    stage_a(1)
-    pl.when(chosen & (slot >= 2))(send_tiles)
-    stage_b(0)
-    stage_b(1)
+    near_tiles(range(10))
+    for c in range(6):
+        far_tiles(range(*CHUNKS[c]))
+        stage_a(c)
+    for c in range(6):
+        stage_f(c)
     rhs_arrived()
-    near_tiles(later_slots)
-    stage_c(0)
-    far_tiles((4, 5))
-    stage_a(2)
-    far_tiles((6, 7))
-    stage_a(3)
-    far_tiles((8, 9))
-    stage_a(4)
-    stage_a(5)
-    stage_c(1)
-    for c in range(2, 6):
+    for c in range(6):
         stage_b(c)
-    stage_e(0)
+    for c in range(6):
+        stage_c(c)
     x_ready(0)
-    first_product(0)
-    stage_e(1)
-    stage_c(2)
-    stage_c(3)
-    first_product(1)
+    for c in range(4):
+        stage_e(c)
+        first_product(c)
+    stage_e(4)
+    stage_e(5)
+    first_product(4)
+    y_copy(0).start()
 
     total = jnp.zeros((T, T), jnp.float32)
     for k in range(16):
-        total = total + W[k, k % 2].astype(jnp.float32)
+        total = total + W[k // 4, k % 4, k % 2].astype(jnp.float32)
     eye = lax.broadcasted_iota(jnp.int32, (T, T), 0) == lax.broadcasted_iota(jnp.int32, (T, T), 1)
     total = jnp.where(eye, total, 0.0)
     trace = jnp.sum(jnp.sum(total, axis=0, keepdims=True), axis=1, keepdims=True)
@@ -317,16 +324,6 @@
     shift_copy = send(shs.at[0], shs.at[1], shs_sem.at[0], shr_sem.at[0], sib)
     shift_copy.start()
 
-    stage_c(4)
-    stage_c(5)
-    stage_e(2)
-    first_product(2)
-    stage_e(3)
-    first_product(3)
-    stage_e(4)
-    stage_e(5)
-    first_product(4)
-
     def both(v):
         s = v[:16] + v[16:]
         return jnp.concatenate([s, s], axis=0)
@@ -343,9 +340,9 @@
     shift = jnp.where(h == 0, shs[0], shs[1])[:1, :1]
 
     def iteration(it, rr):
+        y_copy(it).wait()
         curve = []
         for c, s in enumerate(slabs):
-            y_copy(it, c).wait()
             own, other = Y[h, c], Z[it, c]
             real = jnp.where(h == 0, own, other)
             imag = jnp.where(h == 0, other, own)
@@ -377,7 +374,7 @@
                 for n in range(5):
                     acc = products(it + 1, c, n, acc)
                 Y[:, c] = acc.reshape(2, 32, 256)
-                y_copy(it + 1, c).start()
+            y_copy(it + 1).start()
 
         return new
 
@@ -386,53 +383,67 @@
     dst, arrive = R.at[bl_me, 2 * y + h], orr.at[bl_me, 2 * y + h]
 
     def out_copies():
-        for k in range(16):
-            target = (hb, k, home)
-            yield is_me(*target), target, O.at[k], ors.at[k], k
-
-    for me, target, src, sem, k in out_copies():
+        for n, (dy, dx) in enumerate(FAR_FIRST):
+            row = step_y(step_x(i, dx), dy)
+            target = (hb, row, home)
+            yield (is_me(*target) if dx + dy == 0 else None), target, O.at[row], ors.at[n]
+
+    for k in range(16):
         cols = slice(T * k, T * k + T)
         O[k, 0] = sol[:, cols].astype(jnp.bfloat16)
         O[k, 1] = res[:, cols].astype(jnp.bfloat16)
-        pl.when(jnp.logical_not(me))(lambda: send(src, dst, sem, arrive, target).start())
-        pl.when(me)(lambda: pltpu.make_async_copy(src, dst, arrive).start())
+    for me, target, src, sem in out_copies():
+        go = lambda: send(src, dst, sem, arrive, target).start()
+        if me is None:
+            go()
+        else:
+            pl.when(jnp.logical_not(me))(go)
+            pl.when(me)(lambda: pltpu.make_async_copy(src, dst, arrive).start())
 
     for bl in range(2):
         for g in range(8):
             send(O.at[0], R.at[bl, g], ors.at[0], orr.at[bl, g], sib).wait_recv()
-        for n, out in enumerate((out_s, out_r)):
-            for part in range(2):
-                tile = jnp.concatenate(
-                    [R[bl, g, n, 16 * part:16 * part + 16, :].astype(jnp.float32) for g in range(8)], axis=0)
-                out[bl, part] = tile.T
+    out[...] = R[...]
 
     @pl.when(chosen)
     def _():
         for cond, target, src, sem in tile_copies():
-            when(cond, lambda: send(src, W.at[i, t], sem, zr.at[t], target).wait_send())
+            when(cond, lambda: send(src, W.at[y, x, t], sem, zr.at[t], target).wait_send())
     for u in range(10):
         _, relay, target = route(u)
         pl.when(both_conds(relay, slot_ok(u, i)))(lambda: tile_pass(u, target).wait_send())
     for me, target, src, sem in rhs_copies():
         pl.when(jnp.logical_not(me))(lambda: send(src, B.at[i], sem, br.at[i], target).wait_send())
-    for me, target, src, sem, k in out_copies():
-        pl.when(jnp.logical_not(me))(lambda: send(src, dst, sem, arrive, target).wait_send())
+    for me, target, src, sem in out_copies():
+        when(True if me is None else jnp.logical_not(me), lambda: send(src, dst, sem, arrive, target).wait_send())
     for c in range(6):
         first, second = axes(c)
         def own():
-            for n in range(5):
+            for n in range(2):
                 panel_send(i, c, n, step_x(i, 1)).wait_send()
         when(row_ok(c, i), own)
-        for n, e in enumerate((1, 3, 2)):
-            def peer():
-                for m in range(2):
-                    panel_send(i, c, 5 + 2 * n + m, step_x(i, 1)).wait_send()
-            when(row_ok(c, first(i, e)), peer)
-        for e in range(4):
-            row = first(second(i, forward_side(c, e)), e)
-            when(row_ok(c, row), lambda: panel_send(i, c, 11 + e, step_x(i, 1)).wait_send())
+        for e, part in ((1, 0), (3, 1)):
+            row = first(i, e)
+            when(row_ok(c, row), lambda: panel_send(row, c, 2 + 5 * part, step_x(i, 1), part).wait_send())
+        line = line_of(c, i)
+        def group():
+            for n in (3, 4):
+                group_send(line, c, n, None, 0, step_x(i, 1)).wait_send()
+        when(line_ok(c, line), group)
+        for side, part in ((1, 0), (3, 1)):
+            line = line_of(c, second(i, side))
+            when(line_ok(c, line), lambda: group_send(line, c, 5 + part, part, 0, step_x(i, 1)).wait_send())
     for it in range(ITERS):
         x_copy(it).wait_send()
+
+
+def turn_back(r, out_s, out_r):
+    for bl in range(2):
+        for n, out in enumerate((out_s, out_r)):
+            for part in range(2):
+                tile = jnp.concatenate(
+                    [r[bl, g, n, 16 * part:16 * part + 16, :].astype(jnp.float32) for g in range(8)], axis=0)
+                out[bl, part] = tile.T
 
 
 def local(gamma, rhs):
@@ -440,13 +451,13 @@
     dma = pltpu.SemaphoreType.DMA
     f32, bf16 = jnp.float32, jnp.bfloat16
     shape = jax.ShapeDtypeStruct(rhs.shape, f32)
-    return pl.pallas_call(
+    gathered = pl.pallas_call(
         kernel,
-        out_shape=(shape, shape),
+        out_shape=jax.ShapeDtypeStruct((2, 8, 2, 32, T), bf16),
         in_specs=[pl.BlockSpec(memory_space=pl.ANY)] * 2,
-        out_specs=(vmem, vmem),
+        out_specs=vmem,
         scratch_shapes=[
-            pltpu.VMEM((16, 10, T, T), bf16),
+            pltpu.VMEM((4, 4, 10, T, T), bf16),
             pltpu.VMEM((2, 2, T, T), f32),
             pltpu.VMEM((2, 8, 32, T), f32),
             pltpu.VMEM((16, 32, T), f32),
@@ -461,13 +472,14 @@
             pltpu.VMEM((32, N), f32),
             pltpu.VMEM((16, 2, 32, T), bf16),
             pltpu.VMEM((2, 8, 2, 32, T), bf16),
-            dma((10,)), dma((12,)), dma((10,)), dma((16,)), dma((16,)), dma((16, 6)), dma((6, 15)),
-            dma((ITERS,)), dma((ITERS,)), dma((ITERS, SB)), dma((ITERS, SB)), dma((1,)), dma((1,)),
+            dma((10,)), dma((12,)), dma((10,)), dma((16,)), dma((16,)), dma((16, 6, 2)), dma((6, 4)), dma((6, 8)),
+            dma((ITERS,)), dma((ITERS,)), dma((ITERS,)), dma((ITERS,)), dma((1,)), dma((1,)),
             dma((2, 8)), dma((16,)), dma((1,)),
         ],
         compiler_params=pltpu.CompilerParams(
             collective_id=0, has_side_effects=True, vmem_limit_bytes=60 * 2**20),
     )(gamma, rhs)
+    return pl.pallas_call(turn_back, out_shape=(shape, shape), in_specs=[vmem], out_specs=(vmem, vmem))(gathered)
 
 
 def solution(mesh):

time: 100 us -> 95.2 us (0.952)
  the two profiles are of different devices: /device:TPU:57 before, /device:TPU:1 now
where the time goes in v3:
time: 95.2 us; the launch traced here: 95 us
  Pallas kernels  94.3 us (99%)
    pallas_call x1, Pallas kernels, local(): pl.pallas_call(kernel, out_shape=jax.ShapeDtypeStruct((2, 8, 2, 32, T), b...  92.4 us

profile of v3, /device:TPU:1, one launch (start us, length us, event | category | flops | bytes accessed | tf_op | source)
XLA Modules:
  0.0 95.0 jit_solution(14692927546445318253)
XLA Ops:
  0.6 92.4 %shard_map.41.r = bf16[2,8,2,32,128]{4,3,2,1,0:T(8,128)(2,1)} custom-call(bf16[2,2,128,128]{3,2,1,0:T(8,128)(2,1)} %gamma.1, f32[2,2,128,128]{3,2,1,0:T(8,128)} %rhs.1), custom_call_target="tpu_custom_call" | custom-call | tf_op jit(solution)/shard_map/pallas_call | solution.py:454
  93.1 1.9 %shard_map.42 = (f32[2,2,128,128]{3,2,1,0:T(8,128)}, f32[2,2,128,128]{3,2,1,0:T(8,128)}) custom-call(bf16[2,8,2,32,128]{4,3,2,1,0:T(8,128)(2,1)} %shard_map.41.r), custom_call_target="tpu_custom_call" | custom-call | tf_op jit(solution)/shard_map/pallas_call | solution.py:482

commit v4 on v3

--- a/solution.py
+++ b/solution.py
@@ -25,7 +25,7 @@
     y, x = i // 4, i % 4
     hb, bl_me = (z % 4) // 2, z % 2
     big = i // 2
-    home = (z + 17 - x) % 16
+    home = (z + 17 + y % 2 - x) % 16
 
     fetch = pltpu.make_async_copy(rhs, tile_in, in_sem.at[0])
     fetch.start()
@@ -69,7 +69,7 @@
     greet(1 - h, i, z, False)
 
     mine = jnp.where(h == hb, 1, 0)
-    pl.semaphore_wait(barrier, 33 + mine - mine * jnp.where(x == 1, 1, 0))
+    pl.semaphore_wait(barrier, 33 + mine - mine * jnp.where(x == 1 + y % 2, 1, 0))
 
     def send(src, dst, send_sem, recv_sem, target):
         return pltpu.make_async_remote_copy(
@@ -158,10 +158,10 @@
     def rhs_copies():
         n = 0
         for bl in range(2):
-            xx = (2 * h + bl + 5 - z % 4) % 4
             for yy in range(4):
+                xx = (2 * h + bl + 5 + yy % 2 - z % 4) % 4
                 for q in range(2):
-                    target = (q, 4 * yy + xx, (z + 15 + xx) % 16)
+                    target = (q, 4 * yy + xx, (z + 15 - yy % 2 + xx) % 16)
                     yield is_me(*target), target, bT.at[bl, 2 * yy + q], bs.at[n]
                     n += 1
 
@@ -170,12 +170,10 @@
             pl.when(jnp.logical_not(me))(lambda: send(src, B.at[i], sem, br.at[i], target).start())
             pl.when(me)(lambda: pltpu.make_async_copy(src, B.at[i], br.at[i]).start())
 
-    def panel_send(row, c, n, target_row, part=None):
+    def panel_send(row, c, n, target_row):
         a, b = CHUNKS[c]
-        rows = slice(0, T) if part is None else slice(part * T // 2, (part + 1) * T // 2)
-        ref = W.at[row // 4, row % 4, a:b, rows]
-        arrive = rs.at[row, c, 0 if part is None else part]
-        return send(ref, ref, ss.at[c, n], arrive, (h, target_row, z))
+        ref = W.at[row // 4, row % 4, a:b]
+        return send(ref, ref, ss.at[c, n], rs.at[row, c], (h, target_row, z))
 
     def group_send(line, c, n, part, sem, target_row):
         a, b = CHUNKS[c]
@@ -199,26 +197,15 @@
     def stage_a(c):
         first, _ = axes(c)
         def body():
-            for n, e in enumerate((1, 3)):
+            for n, e in enumerate((1, 3, 2)):
                 panel_send(i, c, n, first(i, e)).start()
         when(row_ok(c, i), body)
 
-    def stage_f(c):
-        first, _ = axes(c)
-        for e, part in ((1, 0), (3, 1)):
-            row = first(i, e)
-            def body():
-                panel_send(row, c, 0, first(i, 1)).wait_recv()
-                panel_send(row, c, 2 + 5 * part, first(i, 4 - e), part).start()
-            when(row_ok(c, row), body)
-
     def stage_b(c):
         first, second = axes(c)
-        row = first(i, 2)
-        def halves():
-            for part in range(2):
-                panel_send(row, c, 0, first(i, 1), part).wait_recv()
-        when(row_ok(c, row), halves)
+        for e in (1, 3, 2):
+            row = first(i, e)
+            when(row_ok(c, row), lambda: panel_send(row, c, 0, first(i, 1)).wait_recv())
         line = line_of(c, i)
         def body():
             group_send(line, c, 3, None, 1, second(i, 1)).start()
@@ -298,8 +285,6 @@
     for c in range(6):
         far_tiles(range(*CHUNKS[c]))
         stage_a(c)
-    for c in range(6):
-        stage_f(c)
     rhs_arrived()
     for c in range(6):
         stage_b(c)
@@ -400,11 +385,6 @@
             pl.when(jnp.logical_not(me))(go)
             pl.when(me)(lambda: pltpu.make_async_copy(src, dst, arrive).start())
 
-    for bl in range(2):
-        for g in range(8):
-            send(O.at[0], R.at[bl, g], ors.at[0], orr.at[bl, g], sib).wait_recv()
-    out[...] = R[...]
-
     @pl.when(chosen)
     def _():
         for cond, target, src, sem in tile_copies():
@@ -414,17 +394,12 @@
         pl.when(both_conds(relay, slot_ok(u, i)))(lambda: tile_pass(u, target).wait_send())
     for me, target, src, sem in rhs_copies():
         pl.when(jnp.logical_not(me))(lambda: send(src, B.at[i], sem, br.at[i], target).wait_send())
-    for me, target, src, sem in out_copies():
-        when(True if me is None else jnp.logical_not(me), lambda: send(src, dst, sem, arrive, target).wait_send())
     for c in range(6):
-        first, second = axes(c)
+        _, second = axes(c)
         def own():
-            for n in range(2):
+            for n in range(3):
                 panel_send(i, c, n, step_x(i, 1)).wait_send()
         when(row_ok(c, i), own)
-        for e, part in ((1, 0), (3, 1)):
-            row = first(i, e)
-            when(row_ok(c, row), lambda: panel_send(row, c, 2 + 5 * part, step_x(i, 1), part).wait_send())
         line = line_of(c, i)
         def group():
             for n in (3, 4):
@@ -435,6 +410,13 @@
             when(line_ok(c, line), lambda: group_send(line, c, 5 + part, part, 0, step_x(i, 1)).wait_send())
     for it in range(ITERS):
         x_copy(it).wait_send()
+
+    for bl in range(2):
+        for g in range(8):
+            send(O.at[0], R.at[bl, g], ors.at[0], orr.at[bl, g], sib).wait_recv()
+    out[...] = R[...]
+    for me, target, src, sem in out_copies():
+        when(True if me is None else jnp.logical_not(me), lambda: send(src, dst, sem, arrive, target).wait_send())
 
 
 def turn_back(r, out_s, out_r):
@@ -472,7 +454,7 @@
             pltpu.VMEM((32, N), f32),
             pltpu.VMEM((16, 2, 32, T), bf16),
             pltpu.VMEM((2, 8, 2, 32, T), bf16),
-            dma((10,)), dma((12,)), dma((10,)), dma((16,)), dma((16,)), dma((16, 6, 2)), dma((6, 4)), dma((6, 8)),
+            dma((10,)), dma((12,)), dma((10,)), dma((16,)), dma((16,)), dma((16, 6)), dma((6, 4)), dma((6, 7)),
             dma((ITERS,)), dma((ITERS,)), dma((ITERS,)), dma((ITERS,)), dma((1,)), dma((1,)),
             dma((2, 8)), dma((16,)), dma((1,)),
         ],

time: 95.2 us -> 90.3 us (0.949)
  the two profiles are of different devices: /device:TPU:1 before, /device:TPU:33 now
where the time goes in v4:
time: 90.3 us; the launch traced here: 90 us
  Pallas kernels  89.4 us (99%)
    pallas_call x1, Pallas kernels, local(): pl.pallas_call(kernel, out_shape=jax.ShapeDtypeStruct((2, 8, 2, 32, T), b...  87.5 us
    pallas_call x1, Pallas kernels, local(): pl.pallas_call(turn_back, out_shape=(shape, shape), in_specs=[vmem], out_...  1.88 us

profile of v4, /device:TPU:33, one launch (start us, length us, event | category | flops | bytes accessed | tf_op | source)
XLA Modules:
  0.0 90.0 jit_solution(12784074257451796258)
XLA Ops:
  0.6 87.5 %shard_map.41.r = bf16[2,8,2,32,128]{4,3,2,1,0:T(8,128)(2,1)} custom-call(bf16[2,2,128,128]{3,2,1,0:T(8,128)(2,1)} %gamma.1, f32[2,2,128,128]{3,2,1,0:T(8,128)} %rhs.1), custom_call_target="tpu_custom_call" | custom-call | tf_op jit(solution)/shard_map/pallas_call | solution.py:436
  88.2 1.9 %shard_map.42 = (f32[2,2,128,128]{3,2,1,0:T(8,128)}, f32[2,2,128,128]{3,2,1,0:T(8,128)}) custom-call(bf16[2,8,2,32,128]{4,3,2,1,0:T(8,128)(2,1)} %shard_map.41.r), custom_call_target="tpu_custom_call" | custom-call | tf_op jit(solution)/shard_map/pallas_call | solution.py:464

commit v5 on v4

--- a/solution.py
+++ b/solution.py
@@ -294,11 +294,6 @@
     for c in range(4):
         stage_e(c)
         first_product(c)
-    stage_e(4)
-    stage_e(5)
-    first_product(4)
-    y_copy(0).start()
-
     total = jnp.zeros((T, T), jnp.float32)
     for k in range(16):
         total = total + W[k // 4, k % 4, k % 2].astype(jnp.float32)
@@ -308,6 +303,11 @@
     shs[0] = jnp.broadcast_to(EPS_REL * trace / N, (8, T))
     shift_copy = send(shs.at[0], shs.at[1], shs_sem.at[0], shr_sem.at[0], sib)
     shift_copy.start()
+
+    stage_e(4)
+    stage_e(5)
+    first_product(4)
+    y_copy(0).start()
 
     def both(v):
         s = v[:16] + v[16:]

time: 90.3 us -> 90.3 us (level)
  no operation moved by 1% of the time
where the time goes in v5:
time: 90.3 us; the launch traced here: 90 us
  Pallas kernels  89.4 us (99%)
    pallas_call x1, Pallas kernels, local(): pl.pallas_call(kernel, out_shape=jax.ShapeDtypeStruct((2, 8, 2, 32, T), b...  87.5 us
    pallas_call x1, Pallas kernels, local(): pl.pallas_call(turn_back, out_shape=(shape, shape), in_specs=[vmem], out_...  1.88 us

profile of v5, /device:TPU:33, one launch (start us, length us, event | category | flops | bytes accessed | tf_op | source)
XLA Modules:
  0.0 90.0 jit_solution(13608901650765741554)
XLA Ops:
  0.6 87.5 %shard_map.41.r = bf16[2,8,2,32,128]{4,3,2,1,0:T(8,128)(2,1)} custom-call(bf16[2,2,128,128]{3,2,1,0:T(8,128)(2,1)} %gamma.1, f32[2,2,128,128]{3,2,1,0:T(8,128)} %rhs.1), custom_call_target="tpu_custom_call" | custom-call | tf_op jit(solution)/shard_map/pallas_call | solution.py:436
  88.2 1.9 %shard_map.42 = (f32[2,2,128,128]{3,2,1,0:T(8,128)}, f32[2,2,128,128]{3,2,1,0:T(8,128)}) custom-call(bf16[2,8,2,32,128]{4,3,2,1,0:T(8,128)(2,1)} %shard_map.41.r), custom_call_target="tpu_custom_call" | custom-call | tf_op jit(solution)/shard_map/pallas_call | solution.py:464
